TPU v7x, 32 devices: a whole 2x2x4 slice. The times are simulated.
32 devices in a mesh: rows: 4 (over z), cols: 8 (over y, x, core).
Axes of the slice: x: 2, y: 2, z: 4, core: 2. Of those that a mesh axis runs over, the one named last changes fastest.
Arguments:
- density: bfloat16 [6144, 6144], P('rows', 'cols')
- points: float32 [1536, 3, 256], P(('rows', 'cols')), may hold values from -1 to 1
- grid_weights: float32 [1536, 256], P(('rows', 'cols')), may hold values from 0.002 to 0.02
- centres: float32 [3, 6144], replicated, may hold values from -1 to 1
- exponents: float32 [6144], replicated, may hold values from 3 to 12
- sig_blocks: int32 [1536, 4], P(('rows', 'cols')), may hold values from 0 to 47, as said below
- live_count: int32 [32], P(('rows', 'cols')), may hold values from 1 to 48, as said below
Outputs:
- xc_diag: float32 [6144, 1536], P('rows', 'cols')
- batch_energy: float32 [1536], P(('rows', 'cols'))
- exc_total: float32 [], replicated
Inputs may be any that keep to these rules, and one draw needn't show every extreme that they name: `sig_blocks`: each row holds 4 different blocks in rising order, all among the 48 // 4 blocks of the batch's row group. `live_count`: some device has all 48 slots in use.
All inputs are finite; a program needn't handle non-finite values.
Results may differ from a plain program's by a relative error of at most 0.0005.
Values may be sent and summed in bfloat16 or wider, within the bound.
A program may use at most 64 MiB of HBM per device.

v0:
```python
import functools
import math

import jax
import jax.numpy as jnp
from jax import lax
from jax.experimental import pallas as pl
from jax.experimental.pallas import tpu as pltpu
from jax.sharding import PartitionSpec as P

BLOCK = 128
slater = 0.7386


def function_terms(c, a):
    cc = c[0:1] * c[0:1] + c[1:2] * c[1:2] + c[2:3] * c[2:3]
    coef = jnp.concatenate([2.0 * a * c, -a, -a * cc, jnp.zeros_like(c)], axis=0)
    hi = coef.astype(jnp.bfloat16).astype(jnp.float32)
    rest = coef - hi
    mid = rest.astype(jnp.bfloat16).astype(jnp.float32)
    lo = rest - mid
    return jnp.concatenate([hi, mid, lo, hi, mid, hi], axis=0)


def point_terms(pts_ref, row):
    x, y, z = (pts_ref[axis, pl.ds(row, 1), :] for axis in range(3))
    r2 = x * x + y * y + z * z
    one = jnp.ones_like(x)
    zero = jnp.zeros_like(x)
    v = jnp.concatenate([x, y, z, r2, one, zero, zero, zero], axis=0)
    hi = v.astype(jnp.bfloat16).astype(jnp.float32)
    rest = v - hi
    mid = rest.astype(jnp.bfloat16).astype(jnp.float32)
    lo = rest - mid
    return jnp.concatenate([hi, hi, hi, mid, mid, lo], axis=0)


def phi_rows(terms_ref, s, feats):
    terms = jnp.concatenate([terms_ref[v] for v in s], axis=0)
    arg = jnp.dot(terms, feats, preferred_element_type=jnp.float32)
    return jnp.exp(arg).astype(jnp.bfloat16)


def exchange_kernel(
    nrows, ncols, nsig, chunks, stride,
    sig_ref, live_ref, sig_rows_ref, dens_ref, pts_ref, w_ref, centres_ref, expo_ref,
    pts_all_ref, pot_all_ref, energy_ref, exc_ref, terms_ref, terms_t_ref,
    diag_ref, phi_ref, rho_ref, ebuf_ref, meta_ref,
    local_sem, ring_send, ring_recv, sib_send, sib_recv,
    pts_send, pts_recv, fan_send, fan_recv, pot_send, pot_recv, pfan_send, pfan_recv, exc_send, exc_recv,
):
    group = lax.axis_index("rows")
    me = lax.axis_index("cols")
    slots, npts = w_ref.shape
    span = diag_ref.shape[0]
    held = dens_ref.shape[2] // BLOCK
    ratio = span // held
    nq = ncols // ratio
    lane, place = me % ratio, me // ratio

    def ring_of(q):
        return q // 2 * 2 + (q % 2 + q // 2) % 2 if nq % 2 == 0 else q

    direction = 1 - 2 * (lane % 2)
    ring = ring_of(place)
    after = ring_of((ring + direction + nq) % nq)
    dist = ((ring - ring_of(group)) * direction + 2 * nq) % nq

    barrier = pltpu.get_barrier_semaphore()
    for j in range(1, ncols):
        pl.semaphore_signal(
            barrier, inc=1, device_id=(group, (me + j) % ncols), device_id_type=pl.DeviceIdType.MESH
        )
    for j in range(1, nrows):
        pl.semaphore_signal(
            barrier, inc=1, device_id=((group + j) % nrows, me), device_id_type=pl.DeviceIdType.MESH
        )

    base = group * span
    for j in range(span):
        at = pl.ds(pl.multiple_of((base + j) * BLOCK, BLOCK), BLOCK)
        made = function_terms(centres_ref[:, at], expo_ref[:, at])
        terms_t_ref[j] = made.astype(jnp.bfloat16)
        terms_ref[j] = made.T.astype(jnp.bfloat16)
    live = live_ref[0].astype(jnp.float32)
    meta_ref[...] = jnp.zeros_like(meta_ref)
    meta_ref[1 : 1 + nsig, 0:slots] = sig_rows_ref[...].astype(jnp.float32)
    meta_ref[1 + nsig : 2 + nsig, :] = jnp.full((1, npts), live, jnp.float32)

    pl.semaphore_wait(barrier, ncols + nrows - 2)

    def remote(src, dst, send, recv, to_row, to_col):
        return pltpu.make_async_remote_copy(
            src_ref=src, dst_ref=dst, send_sem=send, recv_sem=recv,
            device_id=(to_row, to_col), device_id_type=pl.DeviceIdType.MESH,
        )

    @pl.when(dist == 0)
    def _():
        own = [
            pltpu.make_async_copy(
                dens_ref.at[:, :, pl.ds(j * BLOCK, BLOCK)], diag_ref.at[:, lane * held + j], local_sem.at[j]
            )
            for j in range(held)
        ]
        for copy in own:
            copy.start()
        for copy in own:
            copy.wait()

    cuts = chunks // span
    some = held // cuts

    def part(c, which):
        return diag_ref.at[c // cuts, pl.ds(which * held + c % cuts * some, some)]

    def ring_copy(c):
        return remote(part(c, lane), part(c, lane), ring_send.at[c], ring_recv.at[c], group, after * ratio + lane)

    def sib_copy(c, j, which):
        to = place * ratio + (lane + j) % ratio
        return remote(part(c, which), part(c, which), sib_send.at[j - 1, c], sib_recv.at[j - 1, c], group, to)

    per = slots // chunks
    mine = me * stride
    for axis in range(3):
        pts_all_ref[axis, pl.ds(pl.multiple_of(mine, 8), slots), :] = pts_ref[axis]

    def chunk_step(c, carry):
        @pl.when(dist > 0)
        def _():
            ring_copy(c).wait_recv()

        @pl.when(dist < nq - 1)
        def _():
            ring_copy(c).start()

        for j in range(1, ratio):
            sib_copy(c, j, lane).start()
        for u in range(per):
            k = c * per + u
            feats = point_terms(pts_ref, k).astype(jnp.bfloat16)
            s = [jnp.maximum(sig_ref[i, k] - base, 0) for i in range(nsig)]
            at = pl.multiple_of(k * nsig * BLOCK, nsig * BLOCK)
            phi_ref[pl.ds(at, nsig * BLOCK), :] = phi_rows(terms_ref, s, feats)
        return carry

    lax.fori_loop(0, chunks, chunk_step, 0)

    def slab(which):
        return pts_all_ref.at[:, pl.ds(pl.multiple_of(which * stride, 8), slots), :]

    def pts_copy(j, owner):
        to = (me + j * ratio) % ncols
        return remote(slab(owner), slab(owner), pts_send.at[j - 1], pts_recv.at[j - 1], group, to)

    def fan_copy(j, l, owner):
        to = place * ratio + (lane + l) % ratio
        return remote(slab(owner), slab(owner), fan_send.at[l - 1, j], fan_recv.at[l - 1, j], group, to)

    for j in range(1, nq):
        pts_copy(j, me).start()
    for l in range(1, ratio):
        fan_copy(0, l, me).start()

    def drain(c, carry):
        for j in range(1, ratio):
            sib_copy(c, j, (lane + ratio - j) % ratio).wait_recv()
        return carry

    lax.fori_loop(0, chunks, drain, 0)

    def image_rho(k):
        s = [jnp.maximum(sig_ref[i, k] - base, 0) for i in range(nsig)]
        phi = phi_ref[pl.ds(pl.multiple_of(k * nsig * BLOCK, BLOCK), nsig * BLOCK), :]
        dens = jnp.concatenate(
            [jnp.concatenate([diag_ref[s[i], s[j]] for j in range(nsig)], axis=1) for i in range(nsig)], axis=0
        )
        image = jnp.dot(dens, phi, preferred_element_type=jnp.float32)
        prod = phi.astype(jnp.float32) * image
        total = jnp.sum(prod.reshape(nsig * BLOCK // 8, 8, npts), axis=0)
        return jnp.sum(total, axis=0, keepdims=True)

    def image_step(t, carry):
        first = image_rho(2 * t)
        second = image_rho(2 * t + 1)
        rho_ref[pl.ds(2 * t, 1), :] = first
        rho_ref[pl.ds(2 * t + 1, 1), :] = second
        return carry

    half = slots // 4
    lax.fori_loop(0, half, image_step, 0)

    for j in range(1, nq):
        owner = (me + ncols - j * ratio) % ncols
        pts_copy(j, owner).wait_recv()
        for l in range(1, ratio):
            fan_copy(j, l, owner).start()

    lax.fori_loop(half, slots // 2, image_step, 0)

    slot = lax.broadcasted_iota(jnp.int32, (slots, npts), 0).astype(jnp.float32)
    w = w_ref[...] * jnp.clip(live - slot, 0.0, 1.0)
    rho = jnp.maximum(rho_ref[...], 0.0)
    above = rho > 0.0
    root = jnp.where(above, jnp.exp2(jnp.log2(jnp.where(above, rho, 1.0)) * (1.0 / 3.0)), 0.0)
    energy = jnp.sum(w * -slater * rho * root, axis=1, keepdims=True)
    energy_ref[...] = energy
    pot_all_ref[pl.ds(pl.multiple_of(mine, 8), slots), :] = (w * (-4.0 / 3.0 * slater)) * root
    own_sum = jnp.sum(energy, axis=0, keepdims=True)
    tail = lax.broadcasted_iota(jnp.int32, (8, npts), 0)
    pot_all_ref[pl.ds(pl.multiple_of(mine + slots, 8), 8), :] = jnp.where(
        tail == 0, jnp.broadcast_to(own_sum, (8, npts)), meta_ref[...]
    )

    def pot_slab(which):
        return pot_all_ref.at[pl.ds(pl.multiple_of(which * stride, 8), stride), :]

    def pot_copy(j, owner):
        to = (me + j * ratio) % ncols
        return remote(pot_slab(owner), pot_slab(owner), pot_send.at[j - 1], pot_recv.at[j - 1], group, to)

    def pfan_copy(j, l, owner):
        to = place * ratio + (lane + l) % ratio
        return remote(pot_slab(owner), pot_slab(owner), pfan_send.at[l - 1, j], pfan_recv.at[l - 1, j], group, to)

    for j in range(1, nq):
        pot_copy(j, me).start()
    for l in range(1, ratio):
        pfan_copy(0, l, me).start()

    def settle(c, carry):
        @pl.when(dist < nq - 1)
        def _():
            ring_copy(c).wait_send()

        for j in range(1, ratio):
            sib_copy(c, j, lane).wait_send()
        return carry

    lax.fori_loop(0, chunks, settle, 0)
    for j in range(1, nq):
        pts_copy(j, me).wait_send()
    for l in range(1, ratio):
        sibling = place * ratio + (lane + ratio - l) % ratio
        for j in range(nq):
            fan_copy(j, l, (me + ncols - j * ratio) % ncols).wait_send()
            fan_copy(j, l, (sibling + ncols - j * ratio) % ncols).wait_recv()
    for j in range(1, nq):
        owner = (me + ncols - j * ratio) % ncols
        pot_copy(j, owner).wait_recv()
        for l in range(1, ratio):
            pfan_copy(j, l, owner).start()
    for l in range(1, ratio):
        sibling = place * ratio + (lane + ratio - l) % ratio
        for j in range(nq):
            pfan_copy(j, l, (sibling + ncols - j * ratio) % ncols).wait_recv()

    part_sum = jnp.zeros((8, BLOCK), jnp.float32)
    for d in range(ncols):
        part_sum += pot_all_ref[d * stride + slots : d * stride + slots + 1, 0:BLOCK]
    ebuf_ref[group] = part_sum

    def exc_copy(j, owner):
        return remote(ebuf_ref.at[owner], ebuf_ref.at[owner], exc_send.at[j - 1], exc_recv.at[j - 1], (group + j) % nrows, me)

    for j in range(1, nrows):
        exc_copy(j, group).start()
    for j in range(1, nq):
        pot_copy(j, me).wait_send()
    for l in range(1, ratio):
        for j in range(nq):
            pfan_copy(j, l, (me + ncols - j * ratio) % ncols).wait_send()
    for j in range(1, nrows):
        exc_copy(j, (group + nrows - j) % nrows).wait_recv()
    exc = jnp.zeros((8, BLOCK), jnp.float32)
    for g in range(nrows):
        exc += ebuf_ref[g]
    exc_ref[...] = exc
    for j in range(1, nrows):
        exc_copy(j, group).wait_send()


def strip_kernel(nsig, slots, stride, piece, sig_ref, live_ref, col_ref, pts_ref, wpot_ref, terms_ref, terms_t_ref, out_ref, phi_a, phi_b, scaled_a, scaled_b, list_ref):
    strip = out_ref.shape[0]
    npiece = strip // piece
    start = col_ref[0]
    blocks = [(start + q * piece) // BLOCK for q in range(npiece)]
    out_ref[...] = jnp.zeros_like(out_ref)

    def scan_device(d, n):
        def scan_slot(k, n):
            hit = jnp.bool_(False)
            for i in range(nsig):
                v = sig_ref[(d * nsig + i) * slots + k]
                for block in blocks:
                    hit = hit | (v == block)
            list_ref[n] = d * stride + k
            return n + hit.astype(jnp.int32)

        return lax.fori_loop(0, live_ref[d], scan_slot, n)

    total = lax.fori_loop(0, live_ref.shape[0], scan_device, jnp.int32(0))
    for extra in range(3):
        list_ref[total + extra] = 0

    def blocks_of(row):
        d = row // stride
        return [sig_ref[(d * nsig + i) * slots + row - d * stride] for i in range(nsig)]

    own = terms_ref[pl.ds(pl.multiple_of(start, piece), strip), :]

    def make(index, phi_dst, scaled_dst):
        row = list_ref[index]
        valid = index < total
        feats = point_terms(pts_ref, row)
        s = blocks_of(row)
        terms = jnp.concatenate([terms_t_ref[v] for v in s], axis=1)
        arg = jnp.dot(feats.T.astype(jnp.bfloat16), terms, preferred_element_type=jnp.float32)
        phi_dst[...] = jnp.exp(arg).astype(jnp.bfloat16)
        wpot = wpot_ref[pl.ds(row, 1), :]
        arg = jnp.dot(own, feats.astype(jnp.bfloat16), preferred_element_type=jnp.float32)
        phi = jnp.exp(arg).astype(jnp.bfloat16).astype(jnp.float32)
        for q in range(npiece):
            have = jnp.bool_(False)
            for v in s:
                have = have | (v == blocks[q])
            on = (have & valid).astype(jnp.float32)
            rows = phi[q * piece : (q + 1) * piece] * (wpot * on)
            scaled_dst[pl.ds(q * piece, piece), :] = rows.astype(jnp.bfloat16)

    def add(index, phi_src, scaled_src):
        s = blocks_of(list_ref[index])
        delta = jnp.dot(scaled_src[...], phi_src[...], preferred_element_type=jnp.float32)
        for i in range(nsig):
            cols = pl.ds(pl.multiple_of(s[i] * BLOCK, BLOCK), BLOCK)
            out_ref[:, cols] += delta[:, i * BLOCK : (i + 1) * BLOCK]

    make(0, phi_a, scaled_a)

    def step(t, carry):
        make(2 * t + 1, phi_b, scaled_b)
        add(2 * t, phi_a, scaled_a)
        make(2 * t + 2, phi_a, scaled_a)
        add(2 * t + 1, phi_b, scaled_b)
        return carry

    lax.fori_loop(0, (total + 1) // 2, step, 0)


def shards(density, points, grid_weights, centres, exponents, sig_blocks, live_count):
    nrows = lax.axis_size("rows")
    ncols = lax.axis_size("cols")
    group = lax.axis_index("rows")
    col = lax.axis_index("cols")
    nsig = sig_blocks.shape[1]
    slots, _, npts = points.shape
    own_width = density.shape[0]
    span = own_width // BLOCK
    strip = own_width // ncols
    piece = math.gcd(strip, BLOCK)
    ratio = own_width // density.shape[1]
    nq = ncols // ratio
    stride = slots + 8
    held = span // ratio
    chunks = span * (2 if held % 2 == 0 and slots % (2 * span) == 0 else 1)

    vmem = pl.BlockSpec(memory_space=pltpu.VMEM)
    smem = pl.BlockSpec(memory_space=pltpu.SMEM)
    hbm = pl.BlockSpec(memory_space=pltpu.HBM)

    dma = pltpu.SemaphoreType.DMA
    pts_all, pot_all, energy, exc, terms, terms_t = pl.pallas_call(
        functools.partial(exchange_kernel, nrows, ncols, nsig, chunks, stride),
        out_shape=(
            jax.ShapeDtypeStruct((3, ncols * stride, npts), jnp.float32),
            jax.ShapeDtypeStruct((ncols * stride, npts), jnp.float32),
            jax.ShapeDtypeStruct((slots, 1), jnp.float32),
            jax.ShapeDtypeStruct((8, BLOCK), jnp.float32),
            jax.ShapeDtypeStruct((span, BLOCK, 48), jnp.bfloat16),
            jax.ShapeDtypeStruct((span, 48, BLOCK), jnp.bfloat16),
        ),
        in_specs=[smem, smem, vmem, hbm, vmem, vmem, vmem, vmem],
        out_specs=(vmem,) * 6,
        scratch_shapes=[
            pltpu.VMEM((span, span, BLOCK, BLOCK), jnp.bfloat16),
            pltpu.VMEM((slots * nsig * BLOCK, npts), jnp.bfloat16),
            pltpu.VMEM((slots, npts), jnp.float32),
            pltpu.VMEM((nrows, 8, BLOCK), jnp.float32),
            pltpu.VMEM((8, npts), jnp.float32),
            dma((span // ratio,)),
            dma((chunks,)),
            dma((chunks,)),
            dma((max(ratio - 1, 1), chunks)),
            dma((max(ratio - 1, 1), chunks)),
            dma((max(nq - 1, 1),)),
            dma((max(nq - 1, 1),)),
            dma((max(ratio - 1, 1), nq)),
            dma((max(ratio - 1, 1), nq)),
            dma((max(nq - 1, 1),)),
            dma((max(nq - 1, 1),)),
            dma((max(ratio - 1, 1), nq)),
            dma((max(ratio - 1, 1), nq)),
            dma((max(nrows - 1, 1),)),
            dma((max(nrows - 1, 1),)),
        ],
        compiler_params=pltpu.CompilerParams(
            collective_id=0, has_side_effects=True, vmem_limit_bytes=48 * 1024 * 1024
        ),
        name="exchange",
    )(
        sig_blocks.T, live_count, sig_blocks.T, density.reshape(span, BLOCK, -1), points.transpose(1, 0, 2),
        grid_weights, centres, exponents.reshape(1, -1),
    )
    own_energy = energy.reshape(slots)
    tails = pot_all.reshape(ncols, stride, npts)[:, slots : slots + 8]
    sig_all = (tails[:, 1 : 1 + nsig, :slots].astype(jnp.int32) - group * span).reshape(-1)
    live_all = tails[:, 1 + nsig, 0].astype(jnp.int32)

    xc_strip = pl.pallas_call(
        functools.partial(strip_kernel, nsig, slots, stride, piece),
        out_shape=jax.ShapeDtypeStruct((strip, own_width), jnp.float32),
        in_specs=[smem, smem, smem, vmem, vmem, vmem, vmem],
        out_specs=vmem,
        scratch_shapes=[
            pltpu.VMEM((npts, nsig * BLOCK), jnp.bfloat16),
            pltpu.VMEM((npts, nsig * BLOCK), jnp.bfloat16),
            pltpu.VMEM((strip, npts), jnp.bfloat16),
            pltpu.VMEM((strip, npts), jnp.bfloat16),
            pltpu.SMEM((ncols * slots + 8,), jnp.int32),
        ],
        compiler_params=pltpu.CompilerParams(vmem_limit_bytes=32 * 1024 * 1024),
        name="strip",
    )(sig_all, live_all, (col * strip).reshape(1).astype(jnp.int32), pts_all, pot_all, terms.reshape(own_width, -1), terms_t)
    return (xc_strip.T, own_energy, exc[0, 0])


def solution(mesh):
    placed = (
        P("rows", "cols"),
        P(("rows", "cols"), None, None),
        P(("rows", "cols"), None),
        P(),
        P(),
        P(("rows", "cols"), None),
        P(("rows", "cols")),
    )
    return jax.shard_map(
        shards,
        mesh=mesh,
        in_specs=placed,
        out_specs=(P("rows", "cols"), P(("rows", "cols")), P()),
        check_vma=False,
    )
```

profile of v0, /device:TPU:0, one launch (start us, length us, event | category | flops | bytes accessed | tf_op | source)
XLA Modules:
  0.0 120.1 jit_solution(7977661392103394535)
XLA Ops:
  1.3 0.0 copy-start
  1.3 1.7 %copy-done = bf16[1536,768]{1,0:T(8,128)(2,1)S(1)} copy-done((bf16[1536,768]{1,0:T(8,128)(2,1)S(1)}, bf16[1536,768]{1,0:T(8,128)(2,1)}, u32[]{:S(2)}) %copy-start) | copy-done | bytes 2359320
  3.0 0.0 copy-start.1
  3.0 0.9 copy-done.1
  3.9 0.0 copy-start.2
  3.9 0.9 copy-done.2
  4.8 0.0 copy-start.3
  4.8 0.8 copy-done.3
  5.6 0.0 copy-start.4
  5.6 0.7 copy-done.4
  6.3 0.0 copy-start.5
  6.3 0.7 copy-done.5
  7.0 69.0 %exchange.1 = (f32[3,448,256]{2,1,0:T(8,128)S(1)}, f32[448,256]{1,0:T(8,128)S(1)}, f32[48,1]{1,0:T(8,128)S(1)}, f32[8,128]{1,0:T(8,128)S(1)}, bf16[12,128,48]{2,...) custom-call(s32[4,48]{1,0:T(4,128)S(1)} %bitcast.17, s32[1]{0:T(128)S(6)} %copy.13.live_ref, s32[4,48]{1,0:T(4,128)S(1)} %bitcast.18, ...), custom_call_target="tpu_custom_call" | custom-call | tf_op jit(solution)/shard_map/exchange/pallas_call | solution.py:373
  76.0 0.5 slice.14
  76.5 0.6 reduce
  77.2 0.1 copy.12
  77.3 0.1 reshape.31.sig_ref
  77.3 42.7 %strip.1 = f32[192,1536]{1,0:T(8,128)} custom-call(s32[1536]{0:T(1024)S(1)} %reshape.31.sig_ref, s32[8]{0:T(128)S(1)} %convert_bitcast_fusion.live_ref, s32[1]{0:T(128)} %bitcast.6.col_ref, f32[3,448,256]{2,1,0:T(8,128)S(1)} %get-tuple-element.10.pts_ref, f32[448,256]{1,0:T(8,128)S(1)} %get-tuple-element.9.wpot_ref, bf16[1536,48]{1,0:T(8,128)(2,1)S(1)} %bitcast.14, ...), custom_call_target="tpu_custom_call" | custom-call | tf_op jit(solution)/shard_map/strip/pallas_call | solution.py:420
  (3 shorter events, 0.0 us)
Async XLA Ops:
  1.3 1.7 %copy-start = (bf16[1536,768]{1,0:T(8,128)(2,1)S(1)}, bf16[1536,768]{1,0:T(8,128)(2,1)}, u32[]{:S(2)}) copy-start(bf16[1536,768]{1,0:T(8,128)(2,1)} %param.7) | copy-start | bytes 7077892
  3.0 0.9 copy-start.1
  3.9 0.9 copy-start.2
  4.8 0.8 copy-start.3
  5.6 0.7 copy-start.4
  6.3 0.7 copy-start.5
where the time goes:
time: 120 us
  Pallas kernels  112 us (93%)
  local copies, waits for them, and re-layouts  6.36 us (5%)
  between operations  1.31 us (1%)
    pallas_call x1, Pallas kernels, shards(): pl.pallas_call(functools.partial(exchange_kernel, nrows, ncols, nsig, chu...  69 us
    pallas_call x1, Pallas kernels, shards(): pl.pallas_call(functools.partial(strip_kernel, nsig, slots, stride, piece...  42.7 us
    unnamed x13, local copies, waits for them, and re-layouts  5.76 us

commit v1 on v0

--- a/solution.py
+++ b/solution.py
@@ -61,10 +61,13 @@
     def ring_of(q):
         return q // 2 * 2 + (q % 2 + q // 2) % 2 if nq % 2 == 0 else q
 
-    direction = 1 - 2 * (lane % 2)
     ring = ring_of(place)
-    after = ring_of((ring + direction + nq) % nq)
-    dist = ((ring - ring_of(group)) * direction + 2 * nq) % nq
+
+    def after(c):
+        return ring_of((ring + 1 - 2 * (c % 2) + nq) % nq)
+
+    def dist(c):
+        return ((ring - ring_of(group)) * (1 - 2 * (c % 2)) + 2 * nq) % nq
 
     barrier = pltpu.get_barrier_semaphore()
     for j in range(1, ncols):
@@ -95,7 +98,7 @@
             device_id=(to_row, to_col), device_id_type=pl.DeviceIdType.MESH,
         )
 
-    @pl.when(dist == 0)
+    @pl.when(ring == ring_of(group))
     def _():
         own = [
             pltpu.make_async_copy(
@@ -115,7 +118,7 @@
         return diag_ref.at[c // cuts, pl.ds(which * held + c % cuts * some, some)]
 
     def ring_copy(c):
-        return remote(part(c, lane), part(c, lane), ring_send.at[c], ring_recv.at[c], group, after * ratio + lane)
+        return remote(part(c, lane), part(c, lane), ring_send.at[c], ring_recv.at[c], group, after(c) * ratio + lane)
 
     def sib_copy(c, j, which):
         to = place * ratio + (lane + j) % ratio
@@ -127,11 +130,11 @@
         pts_all_ref[axis, pl.ds(pl.multiple_of(mine, 8), slots), :] = pts_ref[axis]
 
     def chunk_step(c, carry):
-        @pl.when(dist > 0)
+        @pl.when(dist(c) > 0)
         def _():
             ring_copy(c).wait_recv()
 
-        @pl.when(dist < nq - 1)
+        @pl.when(dist(c) < nq - 1)
         def _():
             ring_copy(c).start()
 
@@ -230,7 +233,7 @@
         pfan_copy(0, l, me).start()
 
     def settle(c, carry):
-        @pl.when(dist < nq - 1)
+        @pl.when(dist(c) < nq - 1)
         def _():
             ring_copy(c).wait_send()
 

time: 120 us -> 264 us (2.20)
  Pallas kernels: 112 us -> 257 us
    pallas_call x1, Pallas kernels: 69 us -> 218 us  [shards(): pl.pallas_call(functools.partial(exchange_kernel, nrows, ncols, nsig, chu...]
    pallas_call x1, Pallas kernels: 42.7 us -> 39 us  [shards(): pl.pallas_call(functools.partial(strip_kernel, nsig, slots, stride, piece...]
where the time goes in v1:
time: 264 us; the launch traced here: 265 us
  Pallas kernels  257 us (97%)
  local copies, waits for them, and re-layouts  6.36 us (2%)
    pallas_call x1, Pallas kernels, shards(): pl.pallas_call(functools.partial(exchange_kernel, nrows, ncols, nsig, chu...  218 us
    pallas_call x1, Pallas kernels, shards(): pl.pallas_call(functools.partial(strip_kernel, nsig, slots, stride, piece...  39 us
    unnamed x13, local copies, waits for them, and re-layouts  5.76 us

profile of v1, /device:TPU:0, one launch (start us, length us, event | category | flops | bytes accessed | tf_op | source)
XLA Modules:
  0.0 264.9 jit_solution(13301171834136971571)
XLA Ops:
  1.3 0.0 copy-start
  1.3 1.7 copy-done
  3.0 0.0 copy-start.1
  3.0 0.9 copy-done.1
  3.9 0.0 copy-start.2
  3.9 0.9 copy-done.2
  4.8 0.0 copy-start.3
  4.8 0.8 copy-done.3
  5.6 0.0 copy-start.4
  5.6 0.7 copy-done.4
  6.3 0.0 copy-start.5
  6.3 0.7 copy-done.5
  7.0 217.6 %exchange.1 = (f32[3,448,256]{2,1,0:T(8,128)S(1)}, f32[448,256]{1,0:T(8,128)S(1)}, f32[48,1]{1,0:T(8,128)S(1)}, f32[8,128]{1,0:T(8,128)S(1)}, bf16[12,128,48]{2,...) custom-call(s32[4,48]{1,0:T(4,128)S(1)} %bitcast.17, s32[1]{0:T(128)S(6)} %copy.13.live_ref, s32[4,48]{1,0:T(4,128)S(1)} %bitcast.18, ...), custom_call_target="tpu_custom_call" | custom-call | tf_op jit(solution)/shard_map/exchange/pallas_call | solution.py:376
  224.6 0.5 slice.14
  225.1 0.6 reduce
  225.7 0.1 copy.12
  225.8 0.1 reshape.31.sig_ref
  225.9 39.0 %strip.1 = f32[192,1536]{1,0:T(8,128)} custom-call(s32[1536]{0:T(1024)S(1)} %reshape.31.sig_ref, s32[8]{0:T(128)S(1)} %convert_bitcast_fusion.live_ref, s32[1]{0:T(128)} %bitcast.6.col_ref, f32[3,448,256]{2,1,0:T(8,128)S(1)} %get-tuple-element.10.pts_ref, f32[448,256]{1,0:T(8,128)S(1)} %get-tuple-element.9.wpot_ref, bf16[1536,48]{1,0:T(8,128)(2,1)S(1)} %bitcast.14, ...), custom_call_target="tpu_custom_call" | custom-call | tf_op jit(solution)/shard_map/strip/pallas_call | solution.py:423
  (3 shorter events, 0.0 us)
Async XLA Ops:
  1.3 1.7 copy-start
  3.0 0.9 copy-start.1
  3.9 0.9 copy-start.2
  4.8 0.8 copy-start.3
  5.6 0.7 copy-start.4
  6.3 0.7 copy-start.5

commit v2 on v1

--- a/solution.py
+++ b/solution.py
@@ -124,31 +124,45 @@
         to = place * ratio + (lane + j) % ratio
         return remote(part(c, which), part(c, which), sib_send.at[j - 1, c], sib_recv.at[j - 1, c], group, to)
 
-    per = slots // chunks
+    steps = chunks // 2
+    per = slots // steps
     mine = me * stride
     for axis in range(3):
         pts_all_ref[axis, pl.ds(pl.multiple_of(mine, 8), slots), :] = pts_ref[axis]
 
-    def chunk_step(c, carry):
-        @pl.when(dist(c) > 0)
+    def move(t, e):
+        c = 2 * (t - dist(e)) + e
+
+        @pl.when((c >= 0) & (c < chunks))
         def _():
-            ring_copy(c).wait_recv()
-
-        @pl.when(dist(c) < nq - 1)
-        def _():
-            ring_copy(c).start()
-
-        for j in range(1, ratio):
-            sib_copy(c, j, lane).start()
+            @pl.when(dist(e) > 0)
+            def _():
+                ring_copy(c).wait_recv()
+
+            @pl.when(dist(e) < nq - 1)
+            def _():
+                ring_copy(c).start()
+
+            for j in range(1, ratio):
+                sib_copy(c, j, lane).start()
+
+    def late_step(t, carry):
+        move(t, 0)
+        move(t, 1)
+        return carry
+
+    def chunk_step(t, carry):
+        late_step(t, carry)
         for u in range(per):
-            k = c * per + u
+            k = t * per + u
             feats = point_terms(pts_ref, k).astype(jnp.bfloat16)
             s = [jnp.maximum(sig_ref[i, k] - base, 0) for i in range(nsig)]
             at = pl.multiple_of(k * nsig * BLOCK, nsig * BLOCK)
             phi_ref[pl.ds(at, nsig * BLOCK), :] = phi_rows(terms_ref, s, feats)
         return carry
 
-    lax.fori_loop(0, chunks, chunk_step, 0)
+    lax.fori_loop(0, steps, chunk_step, 0)
+    lax.fori_loop(steps, steps + nq - 1, late_step, 0)
 
     def slab(which):
         return pts_all_ref.at[:, pl.ds(pl.multiple_of(which * stride, 8), slots), :]

time: 264 us -> 131 us (0.50)
  the two profiles are of different devices: /device:TPU:0 before, /device:TPU:8 now
where the time goes in v2:
time: 131 us; the launch traced here: 133 us
  Pallas kernels  125 us (95%)
  local copies, waits for them, and re-layouts  6.36 us (5%)
  between operations  1.31 us (1%)
    pallas_call x1, Pallas kernels, shards(): pl.pallas_call(functools.partial(exchange_kernel, nrows, ncols, nsig, chu...  76.8 us
    pallas_call x1, Pallas kernels, shards(): pl.pallas_call(functools.partial(strip_kernel, nsig, slots, stride, piece...  48.2 us
    unnamed x13, local copies, waits for them, and re-layouts  5.76 us

profile of v2, /device:TPU:8, one launch (start us, length us, event | category | flops | bytes accessed | tf_op | source)
XLA Modules:
  0.0 133.3 jit_solution(11257428935329337827)
XLA Ops:
  1.3 0.0 copy-start
  1.3 1.7 %copy-done = bf16[1536,768]{1,0:T(8,128)(2,1)S(1)} copy-done((bf16[1536,768]{1,0:T(8,128)(2,1)S(1)}, bf16[1536,768]{1,0:T(8,128)(2,1)}, u32[]{:S(2)}) %copy-start) | copy-done | bytes 2359320
  3.0 0.0 copy-start.1
  3.0 0.9 copy-done.1
  3.9 0.0 copy-start.2
  3.9 0.9 copy-done.2
  4.8 0.0 copy-start.3
  4.8 0.8 copy-done.3
  5.6 0.0 copy-start.4
  5.6 0.7 copy-done.4
  6.3 0.0 copy-start.5
  6.3 0.7 copy-done.5
  7.0 76.8 %exchange.1 = (f32[3,448,256]{2,1,0:T(8,128)S(1)}, f32[448,256]{1,0:T(8,128)S(1)}, f32[48,1]{1,0:T(8,128)S(1)}, f32[8,128]{1,0:T(8,128)S(1)}, bf16[12,128,48]{2,...) custom-call(s32[4,48]{1,0:T(4,128)S(1)} %bitcast.17, s32[1]{0:T(128)S(6)} %copy.13.live_ref, s32[4,48]{1,0:T(4,128)S(1)} %bitcast.18, ...), custom_call_target="tpu_custom_call" | custom-call | tf_op jit(solution)/shard_map/exchange/pallas_call | solution.py:390
  83.8 0.5 slice.14
  84.3 0.6 reduce
  84.9 0.1 copy.12
  85.0 0.1 reshape.31.sig_ref
  85.1 48.2 %strip.1 = f32[192,1536]{1,0:T(8,128)} custom-call(s32[1536]{0:T(1024)S(1)} %reshape.31.sig_ref, s32[8]{0:T(128)S(1)} %convert_bitcast_fusion.live_ref, s32[1]{0:T(128)} %bitcast.6.col_ref, f32[3,448,256]{2,1,0:T(8,128)S(1)} %get-tuple-element.10.pts_ref, f32[448,256]{1,0:T(8,128)S(1)} %get-tuple-element.9.wpot_ref, bf16[1536,48]{1,0:T(8,128)(2,1)S(1)} %bitcast.14, ...), custom_call_target="tpu_custom_call" | custom-call | tf_op jit(solution)/shard_map/strip/pallas_call | solution.py:437
  (3 shorter events, 0.0 us)
Async XLA Ops:
  1.3 1.7 %copy-start = (bf16[1536,768]{1,0:T(8,128)(2,1)S(1)}, bf16[1536,768]{1,0:T(8,128)(2,1)}, u32[]{:S(2)}) copy-start(bf16[1536,768]{1,0:T(8,128)(2,1)} %param.7) | copy-start | bytes 7077892
  3.0 0.9 copy-start.1
  3.9 0.9 copy-start.2
  4.8 0.8 copy-start.3
  5.6 0.7 copy-start.4
  6.3 0.7 copy-start.5
